TPU v7x, 32 devices: a whole 2x2x4 slice. The times are simulated.
32 devices in a mesh: lat: 4 (over y, x), ma: 8 (over z, core).
Axes of the slice: x: 2, y: 2, z: 4, core: 2. Of those that a mesh axis runs over, the one named last changes fastest.
Arguments:
- fourier: bfloat16 [16, 2, 256, 2560], P(None, None, 'ma', 'lat'), may hold values from -6 to 6
- legendre: bfloat16 [16, 1280, 2, 640], P('ma', 'lat'), may hold values from -0.125 to 0.125
- window: int32 [16], replicated, may hold values from 0 to 639, as said below
- assign: int32 [16], replicated, may hold values from 0 to 15, each once
Outputs:
- coefficients: float32 [16, 2, 640, 256], P('ma', None, 'lat')
Inputs may be any that keep to these rules, and one draw needn't show every extreme that they name: `window`: distinct group numbers; 0 and 639 are always among them. `assign`: every position from 0 to 15 appears once.
All inputs are finite; a program needn't handle non-finite values.
Results may differ from a plain program's by a relative error of at most 0.017.
Values may be sent and summed in bfloat16 or wider, within the bound.
A program may use at most 64 MiB of HBM per device.

v0:
```python
import functools

import jax
import jax.numpy as jnp
from jax import lax
from jax.experimental import pallas as pl
from jax.experimental.pallas import tpu as pltpu
from jax.sharding import PartitionSpec as P

MESH = pl.DeviceIdType.MESH
BF16 = jnp.bfloat16
F32 = jnp.float32


def swapped(value, axis, bit):
    mask = 2**bit
    pairs = [(source, source ^ mask) for source in range(lax.axis_size(axis))]
    return lax.ppermute(value, axis, pairs)


def fold_pairs(latitudes, northern):
    pair_rows = latitudes.shape[3] // 2
    leading_rows = latitudes[:, :, :, :pair_rows]
    trailing_rows = latitudes[:, :, :, pair_rows:]
    outgoing = jnp.where(northern, trailing_rows, leading_rows)
    bit_number = lax.axis_size("lat").bit_length() - 2
    arrived = swapped(outgoing, "lat", bit_number)
    staying = jnp.where(northern, leading_rows, trailing_rows)
    upper_rows = jnp.where(northern, staying, arrived).astype(F32)
    lower_rows = jnp.where(northern, arrived, staying).astype(F32)
    return (
        (upper_rows + lower_rows).astype(BF16),
        (upper_rows - lower_rows).astype(BF16),
    )


def plain_on_device(fourier, legendre, window, assign):
    local_groups = legendre.shape[0]
    lat_count = lax.axis_size("lat")
    northern = lax.axis_index("lat") < lat_count // 2
    count = assign.shape[0]
    chosen = assign[:, None] == lax.iota(jnp.int32, count)[None, :]
    ordered = jnp.einsum(
        "iw,wsfr->isfr", chosen.astype(BF16), fourier, preferred_element_type=F32
    ).astype(BF16)
    gathered = lax.all_to_all(ordered, "ma", split_axis=0, concat_axis=2, tiled=True)
    sym_part, anti_part = fold_pairs(gathered, northern)
    all_ids = jnp.sum(jnp.where(chosen, window[None, :], 0), axis=1)
    group_ids = lax.dynamic_slice_in_dim(
        all_ids, lax.axis_index("ma") * local_groups, local_groups
    )
    column_count = legendre.shape[3]
    wave_total = 2 * column_count
    zero_value = jnp.zeros((), BF16)

    def half_term(parity):
        column = 2 * lax.iota(jnp.int32, column_count) + parity
        upper_slot = (column[None, :] >= wave_total - group_ids[:, None])[:, None, :]
        table_part = legendre[:, :, parity, :]
        masked = jnp.stack(
            [
                jnp.where(upper_slot, zero_value, table_part),
                jnp.where(upper_slot, table_part, zero_value),
            ],
            axis=1,
        )
        leading = sym_part[:, 0] if parity == 0 else anti_part[:, 0]
        flipped = ((group_ids + parity) % 2 == 1)[:, None, None]
        trailing = jnp.where(flipped, anti_part[:, 1], sym_part[:, 1])
        sources = jnp.stack([leading, trailing], axis=1)
        return jnp.einsum("gspk,gsfp->gkf", masked, sources, preferred_element_type=F32)

    partials = jnp.stack([half_term(0), half_term(1)], axis=1)
    return lax.psum_scatter(
        partials.astype(BF16), "lat", scatter_dimension=2, tiled=True
    ).astype(F32)


def fused_kernel(
    lat_n,
    ma_n,
    assign_ref,
    window_ref,
    four_hbm,
    leg_hbm,
    out_hbm,
    out_ref,
    four_ref,
    leg_ref,
    stage,
    recv,
    weight,
    part,
    landed,
    send_sem,
    recv_sem,
    psend_sem,
    precv_sem,
    leg_sem,
    four_sem,
    out_sem,
    here_sem,
):
    groups_here = leg_ref.shape[0]
    fields_here = four_ref.shape[2]
    rows = four_ref.shape[3]
    pair = rows // 2
    body = pair // 128 * 128
    tail = pair - body
    kcols = leg_ref.shape[3]
    block = kcols // lat_n
    hemi = lat_n // 2
    half_ma = ma_n // 2
    half_f = half_ma * fields_here

    lat = lax.axis_index("lat")
    ma = lax.axis_index("ma")
    side = lat // hemi
    mine = side
    partner = lax.rem(lat + hemi, lat_n)
    my_half = ma // half_ma

    rows_copy = pltpu.make_async_copy(four_hbm, four_ref, four_sem)
    rows_copy.start()
    table_copy = pltpu.make_async_copy(leg_hbm, leg_ref, leg_sem)
    table_copy.start()

    far = lax.rem(ma + half_ma, ma_n)
    far_first = (1 - my_half) * half_ma
    near_first = my_half * half_ma
    low = lax.rem(ma, 2)

    barrier = pltpu.get_barrier_semaphore()
    met = 0
    for m in range(half_ma):
        for there in (lat, partner):
            pl.semaphore_signal(
                barrier, inc=1, device_id=(there, far_first + m), device_id_type=MESH
            )
            met += 1
    for r in range(1, lat_n):
        if r != hemi:
            pl.semaphore_signal(
                barrier, inc=1, device_id=(lax.rem(lat + r, lat_n), far), device_id_type=MESH
            )
            met += 1

    def pack(q, g):
        slab = four_ref.at[assign_ref[q * groups_here + g]]
        for t in range(2):
            at, rest = t * (pair + tail), body + t * tail
            stage[g, q, t] = jnp.concatenate(
                [slab[n, :, at : at + body] for n in range(2)]
                + [slab[n, :, rest : rest + tail] for n in range(2)],
                axis=1,
            )

    def row_copy(g, q, own):
        t = mine if own else 1 - mine
        return pltpu.make_async_remote_copy(
            src_ref=stage.at[g, q, t],
            dst_ref=recv.at[g, side, ma],
            send_sem=send_sem.at[g, q, t],
            recv_sem=recv_sem.at[g, side, ma],
            device_id=(lat if own else partner, q),
            device_id_type=MESH,
        )

    def place(hop):
        return hop // 2 * 2 + lax.rem(hop + low, 2)

    def send_far(hop, g):
        q = far_first + place(hop)
        pack(q, g)
        row_copy(g, q, False).start()
        row_copy(g, q, True).start()

    def send_near(hop, g):
        q = near_first + place(hop)
        pack(q, g)
        row_copy(g, q, False).start()

        @pl.when(q != ma)
        def _():
            row_copy(g, q, True).start()

        @pl.when(q == ma)
        def _():
            pltpu.make_async_copy(
                stage.at[g, q, mine], recv.at[g, side, ma], recv_sem.at[g, side, ma]
            ).start()

    def each_hop(step):
        def body_of(hop, c):
            step(hop)
            return c

        lax.fori_loop(0, half_ma, body_of, 0)

    rows_copy.wait()
    pl.semaphore_wait(barrier, met)
    pl.semaphore_signal(here_sem, inc=1, device_id=(lat, far), device_id_type=MESH)
    each_hop(lambda hop: send_far(hop, 0))
    pl.semaphore_wait(here_sem, 1)
    each_hop(lambda hop: send_near(hop, 0))

    def both(hop):
        send_far(hop, 1)
        send_near(hop, 1)

    each_hop(both)
    table_copy.wait()

    ids = [window_ref[assign_ref[ma * groups_here + g]] for g in range(groups_here)]
    for g in range(groups_here):
        for e in range(2):

            def fill(j, c, g=g, e=e):
                start = pl.multiple_of(j * 128, 128)
                table = jnp.concatenate(
                    [
                        leg_ref[g, pl.ds(mine * tail, body), e, pl.ds(start, 128)],
                        leg_ref[g, pl.ds((1 - mine) * body, tail), e, pl.ds(start, 128)],
                    ],
                    axis=0,
                ).astype(F32).T
                k = start + lax.broadcasted_iota(jnp.int32, (128, 1), 0)
                under = 2 * k + e < 2 * kcols - ids[g]
                lower = jnp.where(under, table, 0.0)
                upper = jnp.where(under, 0.0, table)
                weight[g, e, pl.ds(start, 128), :] = jnp.concatenate(
                    [lower[:, :body], upper[:, :body], lower[:, body:], upper[:, body:]],
                    axis=1,
                ).astype(BF16)
                return c

            lax.fori_loop(0, kcols // 128, fill, 0)

    lane = lax.broadcasted_iota(jnp.int32, (1, rows), 1)
    in_upper = ((lane >= body) & (lane < 2 * body)) | (lane >= 2 * body + tail)

    def part_copy(g, h, e, r):
        there = lax.rem(lat + r, lat_n)
        return pltpu.make_async_remote_copy(
            src_ref=part.at[g, h, there, e],
            dst_ref=landed.at[r - 1, g, h, e],
            send_sem=psend_sem.at[r - 1, g, h, e],
            recv_sem=precv_sem.at[r - 1, g, h, e],
            device_id=(there, ma),
            device_id_type=MESH,
        )

    def multiply(g, h):
        def arrive(m, c):
            for ns in range(2):
                piece = recv.at[g, ns, h * half_ma + m]
                pltpu.make_async_copy(piece, piece, recv_sem.at[g, ns, h * half_ma + m]).wait()
            return c

        lax.fori_loop(0, half_ma, arrive, 0)
        north = recv[g, 0, pl.ds(h * half_ma, half_ma)].reshape(half_f, rows).astype(F32)
        south = recv[g, 1, pl.ds(h * half_ma, half_ma)].reshape(half_f, rows).astype(F32)
        for e in range(2):
            odd = lax.rem(ids[g] + e, 2).astype(F32)
            sign = jnp.where(in_upper, 1.0 - 2.0 * odd, 1.0 - 2.0 * e)
            source = (north + sign * south).astype(BF16)
            for r in (*range(1, lat_n), 0):
                d = lax.rem(lat + r, lat_n)
                part[g, h, d, e] = lax.dot_general(
                    weight[g, e, pl.ds(pl.multiple_of(d * block, 16), block), :],
                    source,
                    (((1,), (1,)), ((), ())),
                    preferred_element_type=F32,
                ).astype(BF16)
                if r:
                    part_copy(g, h, e, r).start()

    def out_copy(g, h, e):
        at = pl.multiple_of(h * half_f, 128)
        return pltpu.make_async_copy(
            out_ref.at[g, e, h], out_hbm.at[g, e, :, pl.ds(at, half_f)], out_sem.at[g, e, h]
        )

    def finish(g, h):
        for e in range(2):
            for r in range(1, lat_n):
                part_copy(g, h, e, r).wait_recv()
            total = part[g, h, lat, e].astype(F32)
            for r in range(1, lat_n):
                total = total + landed[r - 1, g, h, e].astype(F32)
            out_ref[g, e, h] = total
            out_copy(g, h, e).start()

    chunks = [(g, (my_half + j) % 2) for g in range(groups_here) for j in range(2)]
    for i, (g, h) in enumerate(chunks):
        multiply(g, h)
        if i:
            finish(*chunks[i - 1])
    finish(*chunks[-1])

    for g in range(groups_here):

        def sent(q, c, g=g):
            row_copy(g, q, False).wait_send()

            @pl.when(q != ma)
            def _():
                row_copy(g, q, True).wait_send()

            return c

        lax.fori_loop(0, ma_n, sent, 0)
    for g, h in chunks:
        for e in range(2):
            for r in range(1, lat_n):
                part_copy(g, h, e, r).wait_send()
            out_copy(g, h, e).wait()


def fused_on_device(fourier, legendre, window, assign):
    lat_n, ma_n = lax.axis_size("lat"), lax.axis_size("ma")
    _, slots, fields_here, rows = fourier.shape
    groups_here, pair, parities, kcols = legendre.shape
    block = kcols // lat_n
    fields = fields_here * ma_n
    smem = pl.BlockSpec(memory_space=pltpu.SMEM)
    hbm = pl.BlockSpec(memory_space=pltpu.HBM)
    dma = pltpu.SemaphoreType.DMA
    return pl.pallas_call(
        functools.partial(fused_kernel, lat_n, ma_n),
        out_shape=jax.ShapeDtypeStruct((groups_here, 2, block, fields), F32),
        in_specs=[smem, smem, hbm, hbm],
        out_specs=hbm,
        scratch_shapes=[
            pltpu.VMEM((groups_here, 2, 2, block, fields // 2), F32),
            pltpu.VMEM(fourier.shape, BF16),
            pltpu.VMEM(legendre.shape, BF16),
            pltpu.VMEM((groups_here, ma_n, 2, fields_here, rows), BF16),
            pltpu.VMEM((groups_here, 2, ma_n, fields_here, rows), BF16),
            pltpu.VMEM((groups_here, 2, kcols, rows), BF16),
            pltpu.VMEM((groups_here, 2, lat_n, 2, block, fields // 2), BF16),
            pltpu.VMEM((lat_n - 1, groups_here, 2, 2, block, fields // 2), BF16),
            dma((groups_here, ma_n, 2)),
            dma((groups_here, 2, ma_n)),
            dma((lat_n - 1, groups_here, 2, 2)),
            dma((lat_n - 1, groups_here, 2, 2)),
            dma,
            dma,
            dma((groups_here, 2, 2)),
            pltpu.SemaphoreType.REGULAR,
        ],
        compiler_params=pltpu.CompilerParams(
            collective_id=0, has_side_effects=True, vmem_limit_bytes=63 * 2**20
        ),
        cost_estimate=pl.CostEstimate(
            flops=8 * groups_here * kcols * rows * fields,
            bytes_accessed=2 * (fourier.size + legendre.size),
            transcendentals=0,
        ),
    )(assign, window, fourier, legendre)


def fits_kernel(mesh, fourier, legendre):
    lat_n, ma_n = mesh.shape["lat"], mesh.shape["ma"]
    fields_here = fourier.shape[2] // ma_n
    pair = legendre.shape[1] // lat_n
    block = legendre.shape[3] // lat_n
    return (
        fourier.shape[1] == 2
        and lat_n == 4
        and ma_n == 8
        and legendre.shape[0] == 2 * ma_n
        and fields_here % 16 == 0
        and (fields_here * ma_n) % 256 == 0
        and (2 * pair) % 128 == 0
        and block % 16 == 0
        and legendre.shape[3] % 128 == 0
    )


def solution(mesh):
    def run(fourier, legendre, window, assign):
        fused = fits_kernel(mesh, fourier, legendre)
        return jax.shard_map(
            fused_on_device if fused else plain_on_device,
            mesh=mesh,
            in_specs=(P(None, None, "ma", "lat"), P("ma", "lat", None, None), P(), P()),
            out_specs=P("ma", None, "lat", None),
            check_vma=False,
        )(fourier, legendre, window, assign)

    return run
```

profile of v0, /device:TPU:25, one launch (start us, length us, event | category | flops | bytes accessed | tf_op | source)
XLA Modules:
  0.0 46.3 jit_solution(13816194353242666255)
XLA Ops:
  0.0 44.3 %shard_map.46 = f32[2,2,160,256]{3,2,1,0:T(8,128)} custom-call(s32[16]{0:T(128)} %assign_ref.1, s32[16]{0:T(128)} %window_ref.1, bf16[16,2,32,640]{3,2,1,0:T(8,128)(2,1)} %four_hbm.1, bf16[2,320,2,640]{3,2,1,0:T(2,128)(2,1)} %leg_hbm.1), custom_call_target="tpu_custom_call" | custom-call | flops 1677721600 | bytes 2949120 | tf_op jit(solution)/shard_map/pallas_call | solution.py:329
  44.3 2.0 %copy.6 = f32[2,2,160,256]{3,2,1,0:T(8,128)} copy(f32[2,2,160,256]{3,2,1,0:T(8,128)} %shard_map.46) | data formatting | bytes 1310720
where the time goes:
time: 46.6 us; the launch traced here: 46.3 us
  Pallas kernels  44.3 us (95%)
  local copies, waits for them, and re-layouts  1.98 us (4%)
    pallas_call x1, Pallas kernels, fused_on_device(): pl.pallas_call(functools.partial(fused_kernel, lat_n, ma_n), out_shape=ja...  44.3 us
    unnamed x1, local copies, waits for them, and re-layouts  1.98 us

commit v1 on v0

--- a/solution.py
+++ b/solution.py
@@ -79,26 +79,26 @@
 def fused_kernel(
     lat_n,
     ma_n,
+    assign_hbm,
+    window_hbm,
+    four_hbm,
+    leg_hbm,
+    out_ref,
     assign_ref,
     window_ref,
-    four_hbm,
-    leg_hbm,
-    out_hbm,
-    out_ref,
     four_ref,
     leg_ref,
     stage,
     recv,
     weight,
     part,
-    landed,
+    relay,
     send_sem,
     recv_sem,
     psend_sem,
     precv_sem,
-    leg_sem,
-    four_sem,
-    out_sem,
+    own_sem,
+    load_sem,
     here_sem,
 ):
     groups_here = leg_ref.shape[0]
@@ -120,10 +120,15 @@
     partner = lax.rem(lat + hemi, lat_n)
     my_half = ma // half_ma
 
-    rows_copy = pltpu.make_async_copy(four_hbm, four_ref, four_sem)
+    beside = lat + 1 - 2 * lax.rem(lat, 2)
+    across = lax.rem(beside + hemi, lat_n)
+
+    assign_copy = pltpu.make_async_copy(assign_hbm, assign_ref, load_sem.at[0])
+    window_copy = pltpu.make_async_copy(window_hbm, window_ref, load_sem.at[1])
+    rows_copy = pltpu.make_async_copy(four_hbm, four_ref, load_sem.at[2])
+    table_copy = pltpu.make_async_copy(leg_hbm, leg_ref, load_sem.at[3])
+    assign_copy.start()
     rows_copy.start()
-    table_copy = pltpu.make_async_copy(leg_hbm, leg_ref, leg_sem)
-    table_copy.start()
 
     far = lax.rem(ma + half_ma, ma_n)
     far_first = (1 - my_half) * half_ma
@@ -138,12 +143,11 @@
                 barrier, inc=1, device_id=(there, far_first + m), device_id_type=MESH
             )
             met += 1
-    for r in range(1, lat_n):
-        if r != hemi:
-            pl.semaphore_signal(
-                barrier, inc=1, device_id=(lax.rem(lat + r, lat_n), far), device_id_type=MESH
-            )
-            met += 1
+    for there in (beside, across):
+        pl.semaphore_signal(barrier, inc=1, device_id=(there, far), device_id_type=MESH)
+        met += 1
+    window_copy.start()
+    table_copy.start()
 
     def pack(q, g):
         slab = four_ref.at[assign_ref[q * groups_here + g]]
@@ -197,18 +201,16 @@
 
         lax.fori_loop(0, half_ma, body_of, 0)
 
+    assign_copy.wait()
     rows_copy.wait()
     pl.semaphore_wait(barrier, met)
     pl.semaphore_signal(here_sem, inc=1, device_id=(lat, far), device_id_type=MESH)
     each_hop(lambda hop: send_far(hop, 0))
     pl.semaphore_wait(here_sem, 1)
     each_hop(lambda hop: send_near(hop, 0))
-
-    def both(hop):
-        send_far(hop, 1)
-        send_near(hop, 1)
-
-    each_hop(both)
+    each_hop(lambda hop: send_near(hop, 1))
+    each_hop(lambda hop: send_far(hop, 1))
+    window_copy.wait()
     table_copy.wait()
 
     ids = [window_ref[assign_ref[ma * groups_here + g]] for g in range(groups_here)]
@@ -239,23 +241,45 @@
     lane = lax.broadcasted_iota(jnp.int32, (1, rows), 1)
     in_upper = ((lane >= body) & (lane < 2 * body)) | (lane >= 2 * body + tail)
 
-    def part_copy(g, h, e, r):
-        there = lax.rem(lat + r, lat_n)
+    chunks = [(g, j) for j in range(2) for g in range(groups_here)]
+    last = len(chunks) - 1
+
+    def remote(c, e, k, source, target, there):
         return pltpu.make_async_remote_copy(
-            src_ref=part.at[g, h, there, e],
-            dst_ref=landed.at[r - 1, g, h, e],
-            send_sem=psend_sem.at[r - 1, g, h, e],
-            recv_sem=precv_sem.at[r - 1, g, h, e],
+            src_ref=source,
+            dst_ref=target,
+            send_sem=psend_sem.at[c, e, k],
+            recv_sem=precv_sem.at[c, e, k],
             device_id=(there, ma),
             device_id_type=MESH,
         )
 
-    def multiply(g, h):
-        def arrive(m, c):
+    def own_copy(c, e):
+        return pltpu.make_async_copy(
+            part.at[c, lat, e], out_ref.at[0, c, e], own_sem.at[c, e]
+        )
+
+    def beside_copy(c, e):
+        return remote(c, e, 0, part.at[c, beside, e], out_ref.at[1, c, e], beside)
+
+    def across_copy(c, e):
+        source = part.at[c, across, e]
+        if c == last:
+            return remote(c, e, 1, source, out_ref.at[3, c, e], across)
+        return remote(c, e, 1, source, relay.at[c, e], beside)
+
+    def partner_copy(c, e):
+        return remote(c, e, 2, part.at[c, partner, e], out_ref.at[2, c, e], partner)
+
+    def multiply(c):
+        g, j = chunks[c]
+        h = lax.rem(my_half + j, 2)
+
+        def arrive(m, v):
             for ns in range(2):
                 piece = recv.at[g, ns, h * half_ma + m]
                 pltpu.make_async_copy(piece, piece, recv_sem.at[g, ns, h * half_ma + m]).wait()
-            return c
+            return v
 
         lax.fori_loop(0, half_ma, arrive, 0)
         north = recv[g, 0, pl.ds(h * half_ma, half_ma)].reshape(half_f, rows).astype(F32)
@@ -264,39 +288,43 @@
             odd = lax.rem(ids[g] + e, 2).astype(F32)
             sign = jnp.where(in_upper, 1.0 - 2.0 * odd, 1.0 - 2.0 * e)
             source = (north + sign * south).astype(BF16)
-            for r in (*range(1, lat_n), 0):
-                d = lax.rem(lat + r, lat_n)
-                part[g, h, d, e] = lax.dot_general(
+
+            def product(d):
+                part[c, d, e] = lax.dot_general(
                     weight[g, e, pl.ds(pl.multiple_of(d * block, 16), block), :],
                     source,
                     (((1,), (1,)), ((), ())),
                     preferred_element_type=F32,
                 ).astype(BF16)
-                if r:
-                    part_copy(g, h, e, r).start()
-
-    def out_copy(g, h, e):
-        at = pl.multiple_of(h * half_f, 128)
-        return pltpu.make_async_copy(
-            out_ref.at[g, e, h], out_hbm.at[g, e, :, pl.ds(at, half_f)], out_sem.at[g, e, h]
-        )
-
-    def finish(g, h):
+
+            product(across)
+            across_copy(c, e).start()
+            product(beside)
+            beside_copy(c, e).start()
+            product(partner)
+            if c == last:
+                partner_copy(c, e).start()
+            product(lat)
+            own_copy(c, e).start()
+
+    def pass_on(c):
         for e in range(2):
-            for r in range(1, lat_n):
-                part_copy(g, h, e, r).wait_recv()
-            total = part[g, h, lat, e].astype(F32)
-            for r in range(1, lat_n):
-                total = total + landed[r - 1, g, h, e].astype(F32)
-            out_ref[g, e, h] = total
-            out_copy(g, h, e).start()
-
-    chunks = [(g, (my_half + j) % 2) for g in range(groups_here) for j in range(2)]
-    for i, (g, h) in enumerate(chunks):
-        multiply(g, h)
-        if i:
-            finish(*chunks[i - 1])
-    finish(*chunks[-1])
+            across_copy(c, e).wait_recv()
+            total = part[c, partner, e].astype(F32) + relay[c, e].astype(F32)
+            part[c, partner, e] = total.astype(BF16)
+            partner_copy(c, e).start()
+
+    for c in range(last + 1):
+        multiply(c)
+        if 0 < c:
+            pass_on(c - 1)
+
+    for c in range(last + 1):
+        for e in range(2):
+            beside_copy(c, e).wait_recv()
+            if c == last:
+                across_copy(c, e).wait_recv()
+            partner_copy(c, e).wait_recv()
 
     for g in range(groups_here):
 
@@ -310,11 +338,45 @@
             return c
 
         lax.fori_loop(0, ma_n, sent, 0)
-    for g, h in chunks:
+    for c in range(last + 1):
         for e in range(2):
-            for r in range(1, lat_n):
-                part_copy(g, h, e, r).wait_send()
-            out_copy(g, h, e).wait()
+            beside_copy(c, e).wait_send()
+            across_copy(c, e).wait_send()
+            partner_copy(c, e).wait_send()
+            own_copy(c, e).wait()
+
+
+def sum_kernel(ma_n, parts_ref, out_hbm, held, total, in_sem, out_sem):
+    chunk_count = held.shape[1]
+    groups_here = chunk_count // 2
+    half_f = held.shape[4]
+    my_half = lax.axis_index("ma") // (ma_n // 2)
+
+    def fetch(c):
+        terms = 4 if c == chunk_count - 1 else 3
+        return pltpu.make_async_copy(
+            parts_ref.at[pl.ds(0, terms), c], held.at[pl.ds(0, terms), c], in_sem.at[c]
+        )
+
+    def store(c):
+        at = pl.multiple_of(lax.rem(my_half + c // groups_here, 2) * half_f, 128)
+        return pltpu.make_async_copy(
+            total.at[c],
+            out_hbm.at[c % groups_here, :, :, pl.ds(at, half_f)],
+            out_sem.at[c],
+        )
+
+    for c in range(chunk_count):
+        fetch(c).start()
+    for c in range(chunk_count):
+        fetch(c).wait()
+        value = held[0, c].astype(F32)
+        for k in range(1, 4 if c == chunk_count - 1 else 3):
+            value = value + held[k, c].astype(F32)
+        total[c] = value
+        store(c).start()
+    for c in range(chunk_count):
+        store(c).wait()
 
 
 def fused_on_device(fourier, legendre, window, assign):
@@ -323,41 +385,59 @@
     groups_here, pair, parities, kcols = legendre.shape
     block = kcols // lat_n
     fields = fields_here * ma_n
-    smem = pl.BlockSpec(memory_space=pltpu.SMEM)
+    chunks = 2 * groups_here
+    half_f = fields // 2
     hbm = pl.BlockSpec(memory_space=pltpu.HBM)
+    anywhere = pl.BlockSpec(memory_space=pl.ANY)
     dma = pltpu.SemaphoreType.DMA
-    return pl.pallas_call(
+    parts = pl.pallas_call(
         functools.partial(fused_kernel, lat_n, ma_n),
-        out_shape=jax.ShapeDtypeStruct((groups_here, 2, block, fields), F32),
-        in_specs=[smem, smem, hbm, hbm],
-        out_specs=hbm,
+        out_shape=jax.ShapeDtypeStruct((4, chunks, 2, block, half_f), BF16),
+        in_specs=[hbm, hbm, hbm, hbm],
+        out_specs=anywhere,
         scratch_shapes=[
-            pltpu.VMEM((groups_here, 2, 2, block, fields // 2), F32),
+            pltpu.SMEM(assign.shape, jnp.int32),
+            pltpu.SMEM(window.shape, jnp.int32),
             pltpu.VMEM(fourier.shape, BF16),
             pltpu.VMEM(legendre.shape, BF16),
             pltpu.VMEM((groups_here, ma_n, 2, fields_here, rows), BF16),
             pltpu.VMEM((groups_here, 2, ma_n, fields_here, rows), BF16),
             pltpu.VMEM((groups_here, 2, kcols, rows), BF16),
-            pltpu.VMEM((groups_here, 2, lat_n, 2, block, fields // 2), BF16),
-            pltpu.VMEM((lat_n - 1, groups_here, 2, 2, block, fields // 2), BF16),
+            pltpu.VMEM((chunks, lat_n, 2, block, half_f), BF16),
+            pltpu.VMEM((chunks - 1, 2, block, half_f), BF16),
             dma((groups_here, ma_n, 2)),
             dma((groups_here, 2, ma_n)),
-            dma((lat_n - 1, groups_here, 2, 2)),
-            dma((lat_n - 1, groups_here, 2, 2)),
-            dma,
-            dma,
-            dma((groups_here, 2, 2)),
+            dma((chunks, 2, 3)),
+            dma((chunks, 2, 3)),
+            dma((chunks, 2)),
+            dma((4,)),
             pltpu.SemaphoreType.REGULAR,
         ],
         compiler_params=pltpu.CompilerParams(
-            collective_id=0, has_side_effects=True, vmem_limit_bytes=63 * 2**20
+            collective_id=0, has_side_effects=True, vmem_limit_bytes=24 * 2**20
         ),
         cost_estimate=pl.CostEstimate(
             flops=8 * groups_here * kcols * rows * fields,
             bytes_accessed=2 * (fourier.size + legendre.size),
             transcendentals=0,
         ),
-    )(assign, window, fourier, legendre)
+    )(*(pltpu.with_memory_space_constraint(x, pltpu.HBM) for x in (assign, window, fourier, legendre)))
+    return pl.pallas_call(
+        functools.partial(sum_kernel, ma_n),
+        out_shape=jax.ShapeDtypeStruct((groups_here, 2, block, fields), F32),
+        in_specs=[anywhere],
+        out_specs=hbm,
+        scratch_shapes=[
+            pltpu.VMEM(parts.shape, BF16),
+            pltpu.VMEM((chunks, 2, block, half_f), F32),
+            dma((chunks,)),
+            dma((chunks,)),
+        ],
+        compiler_params=pltpu.CompilerParams(vmem_limit_bytes=16 * 2**20),
+        cost_estimate=pl.CostEstimate(
+            flops=parts.size, bytes_accessed=4 * parts.size, transcendentals=0
+        ),
+    )(parts)
 
 
 def fits_kernel(mesh, fourier, legendre):

time: 46.6 us -> 43.7 us (0.938)
  local copies, waits for them, and re-layouts: 1.98 us -> 0 us
  Pallas kernels: 44.3 us -> 43.5 us
    pallas_call x1, Pallas kernels: 44.3 us -> 42.2 us  [fused_on_device(): pl.pallas_call(functools.partial(fused_kernel, lat_n, ma_n), out_shape=ja...]
    unnamed x1 -> x0, local copies, waits for them, and re-layouts: 1.98 us -> none
    pallas_call x0 -> x1, Pallas kernels: none -> 1.3 us  [fused_on_device(): pl.pallas_call(functools.partial(sum_kernel, ma_n), out_shape=jax.ShapeDt...]
where the time goes in v1:
time: 43.7 us; the launch traced here: 43.5 us
  Pallas kernels  43.5 us (100%)
    pallas_call x1, Pallas kernels, fused_on_device(): pl.pallas_call(functools.partial(fused_kernel, lat_n, ma_n), out_shape=ja...  42.2 us
    pallas_call x1, Pallas kernels, fused_on_device(): pl.pallas_call(functools.partial(sum_kernel, ma_n), out_shape=jax.ShapeDt...  1.3 us

profile of v1, /device:TPU:25, one launch (start us, length us, event | category | flops | bytes accessed | tf_op | source)
XLA Modules:
  0.0 43.5 jit_solution(17292161278531244671)
XLA Ops:
  0.0 42.2 %shard_map.46.parts_ref = bf16[4,4,2,160,128]{4,3,2,1,0:T(8,128)(2,1)S(1)} custom-call(s32[16]{0:T(128)} %assign_hbm.1, s32[16]{0:T(128)} %window_hbm.1, bf16[16,2,32,640]{3,2,1,0:T(8,128)(2,1)} %four_hbm.1, bf16[2,320,2,640]{3,2,1,0:T(2,128)(2,1)} %leg_hbm.1), custom_call_target="tpu_custom_call" | custom-call | flops 1677721600 | bytes 2949120 | tf_op jit(solution)/shard_map/pallas_call | solution.py:393
  42.3 1.3 %shard_map.47 = f32[2,2,160,256]{3,2,1,0:T(8,128)} custom-call(bf16[4,4,2,160,128]{4,3,2,1,0:T(8,128)(2,1)S(1)} %shard_map.46.parts_ref), custom_call_target="tpu_custom_call" | custom-call | flops 655360 | bytes 2621440 | tf_op jit(solution)/shard_map/pallas_call | solution.py:425

commit v2 on v1

--- a/solution.py
+++ b/solution.py
@@ -271,41 +271,74 @@
     def partner_copy(c, e):
         return remote(c, e, 2, part.at[c, partner, e], out_ref.at[2, c, e], partner)
 
+    def arrive(g, m):
+        for ns in range(2):
+            piece = recv.at[g, ns, m]
+            pltpu.make_async_copy(piece, piece, recv_sem.at[g, ns, m]).wait()
+
+    def source_of(g, e, north, south):
+        odd = lax.rem(ids[g] + e, 2).astype(F32)
+        sign = jnp.where(in_upper, 1.0 - 2.0 * odd, 1.0 - 2.0 * e)
+        return (north + sign * south).astype(BF16)
+
+    def product(g, e, d, source):
+        return lax.dot_general(
+            weight[g, e, pl.ds(pl.multiple_of(d * block, 16), block), :],
+            source,
+            (((1,), (1,)), ((), ())),
+            preferred_element_type=F32,
+        )
+
+    def send_parts(c, k, value):
+        for d in (across, beside, partner, lat):
+            part[c, d, k] = value(d).astype(BF16)
+            if d is across:
+                across_copy(c, k).start()
+            elif d is beside:
+                beside_copy(c, k).start()
+            elif d is lat:
+                own_copy(c, k).start()
+            elif c == last:
+                partner_copy(c, k).start()
+
     def multiply(c):
         g, j = chunks[c]
-        h = lax.rem(my_half + j, 2)
-
-        def arrive(m, v):
-            for ns in range(2):
-                piece = recv.at[g, ns, h * half_ma + m]
-                pltpu.make_async_copy(piece, piece, recv_sem.at[g, ns, h * half_ma + m]).wait()
+        first = lax.rem(my_half + j, 2) * half_ma
+
+        def each(m, v):
+            arrive(g, first + m)
             return v
 
-        lax.fori_loop(0, half_ma, arrive, 0)
-        north = recv[g, 0, pl.ds(h * half_ma, half_ma)].reshape(half_f, rows).astype(F32)
-        south = recv[g, 1, pl.ds(h * half_ma, half_ma)].reshape(half_f, rows).astype(F32)
+        lax.fori_loop(0, half_ma, each, 0)
+        north = recv[g, 0, pl.ds(first, half_ma)].reshape(half_f, rows).astype(F32)
+        south = recv[g, 1, pl.ds(first, half_ma)].reshape(half_f, rows).astype(F32)
         for e in range(2):
-            odd = lax.rem(ids[g] + e, 2).astype(F32)
-            sign = jnp.where(in_upper, 1.0 - 2.0 * odd, 1.0 - 2.0 * e)
-            source = (north + sign * south).astype(BF16)
-
-            def product(d):
-                part[c, d, e] = lax.dot_general(
-                    weight[g, e, pl.ds(pl.multiple_of(d * block, 16), block), :],
-                    source,
-                    (((1,), (1,)), ((), ())),
-                    preferred_element_type=F32,
-                ).astype(BF16)
-
-            product(across)
-            across_copy(c, e).start()
-            product(beside)
-            beside_copy(c, e).start()
-            product(partner)
-            if c == last:
-                partner_copy(c, e).start()
-            product(lat)
-            own_copy(c, e).start()
+            source = source_of(g, e, north, south)
+            send_parts(c, e, lambda d, e=e, source=source: product(g, e, d, source))
+
+    even_lane = lax.broadcasted_iota(jnp.int32, (1, half_f), 1) < half_f // 2
+
+    def multiply_last():
+        g = chunks[last][0]
+        for k in range(2):
+            core = lax.rem(low + k, 2)
+            members = [far_first + 2 * n + core for n in range(half_ma // 2)]
+            for m in members:
+                arrive(g, m)
+            north, south = (
+                jnp.concatenate([recv[g, ns, m] for m in members], axis=0).astype(F32)
+                for ns in range(2)
+            )
+            source = jnp.concatenate(
+                [source_of(g, e, north, south) for e in range(2)], axis=0
+            )
+            send_parts(
+                last,
+                k,
+                lambda d, source=source: jnp.where(
+                    even_lane, product(g, 0, d, source), product(g, 1, d, source)
+                ),
+            )
 
     def pass_on(c):
         for e in range(2):
@@ -314,10 +347,13 @@
             part[c, partner, e] = total.astype(BF16)
             partner_copy(c, e).start()
 
-    for c in range(last + 1):
-        multiply(c)
-        if 0 < c:
-            pass_on(c - 1)
+    multiply(0)
+    multiply(1)
+    pass_on(0)
+    pass_on(1)
+    multiply(2)
+    pass_on(2)
+    multiply_last()
 
     for c in range(last + 1):
         for e in range(2):
@@ -373,7 +409,24 @@
         value = held[0, c].astype(F32)
         for k in range(1, 4 if c == chunk_count - 1 else 3):
             value = value + held[k, c].astype(F32)
-        total[c] = value
+        if c < chunk_count - 1:
+            total[c] = value
+        else:
+            swap = lax.rem(lax.axis_index("ma"), 2) == 1
+            lower = jnp.where(swap, value[1], value[0])
+            upper = jnp.where(swap, value[0], value[1])
+            width = half_f // 4
+            for e in range(2):
+                at = 2 * e * width
+                total[c, e] = jnp.concatenate(
+                    [
+                        lower[:, at : at + width],
+                        upper[:, at : at + width],
+                        lower[:, at + width : at + 2 * width],
+                        upper[:, at + width : at + 2 * width],
+                    ],
+                    axis=1,
+                )
         store(c).start()
     for c in range(chunk_count):
         store(c).wait()

time: 43.7 us -> 40.9 us (0.936)
  Pallas kernels: 43.5 us -> 40.7 us
    pallas_call x1, Pallas kernels: 42.2 us -> 39.3 us  [fused_on_device(): pl.pallas_call(functools.partial(fused_kernel, lat_n, ma_n), out_shape=ja...]
where the time goes in v2:
time: 40.9 us; the launch traced here: 40.7 us
  Pallas kernels  40.7 us (100%)
    pallas_call x1, Pallas kernels, fused_on_device(): pl.pallas_call(functools.partial(fused_kernel, lat_n, ma_n), out_shape=ja...  39.3 us
    pallas_call x1, Pallas kernels, fused_on_device(): pl.pallas_call(functools.partial(sum_kernel, ma_n), out_shape=jax.ShapeDt...  1.42 us

profile of v2, /device:TPU:25, one launch (start us, length us, event | category | flops | bytes accessed | tf_op | source)
XLA Modules:
  0.0 40.7 jit_solution(5694816340526758807)
XLA Ops:
  0.0 39.3 %shard_map.46.parts_ref = bf16[4,4,2,160,128]{4,3,2,1,0:T(8,128)(2,1)S(1)} custom-call(s32[16]{0:T(128)} %assign_hbm.1, s32[16]{0:T(128)} %window_hbm.1, bf16[16,2,32,640]{3,2,1,0:T(8,128)(2,1)} %four_hbm.1, bf16[2,320,2,640]{3,2,1,0:T(2,128)(2,1)} %leg_hbm.1), custom_call_target="tpu_custom_call" | custom-call | flops 1677721600 | bytes 2949120 | tf_op jit(solution)/shard_map/pallas_call | solution.py:446
  39.3 1.4 %shard_map.47 = f32[2,2,160,256]{3,2,1,0:T(8,128)} custom-call(bf16[4,4,2,160,128]{4,3,2,1,0:T(8,128)(2,1)S(1)} %shard_map.46.parts_ref), custom_call_target="tpu_custom_call" | custom-call | flops 655360 | bytes 2621440 | tf_op jit(solution)/shard_map/pallas_call | solution.py:478

commit v3 on v2

--- a/solution.py
+++ b/solution.py
@@ -83,6 +83,7 @@
     window_hbm,
     four_hbm,
     leg_hbm,
+    sums_ref,
     out_ref,
     assign_ref,
     window_ref,
@@ -93,13 +94,17 @@
     weight,
     part,
     relay,
+    landed,
+    total,
     send_sem,
     recv_sem,
     psend_sem,
     precv_sem,
     own_sem,
+    sum_sem,
     load_sem,
     here_sem,
+    late_sem,
 ):
     groups_here = leg_ref.shape[0]
     fields_here = four_ref.shape[2]
@@ -135,17 +140,30 @@
     near_first = my_half * half_ma
     low = lax.rem(ma, 2)
 
+    chip = lax.rem(ma // 2, 2)
+    facing = far_first + 2 * chip
+    other = far_first + 2 * (1 - chip)
+
+    def signal(semaphore, there, q):
+        pl.semaphore_signal(semaphore, inc=1, device_id=(there, q), device_id_type=MESH)
+
+    def signal_chip(semaphore, first):
+        for m in range(2):
+            for there in (lat, partner):
+                signal(semaphore, there, first + m)
+
+    def signal_rest(semaphore):
+        signal_chip(semaphore, other)
+        for there in (beside, across):
+            signal(semaphore, there, far)
+
     barrier = pltpu.get_barrier_semaphore()
-    met = 0
-    for m in range(half_ma):
-        for there in (lat, partner):
-            pl.semaphore_signal(
-                barrier, inc=1, device_id=(there, far_first + m), device_id_type=MESH
-            )
-            met += 1
-    for there in (beside, across):
-        pl.semaphore_signal(barrier, inc=1, device_id=(there, far), device_id_type=MESH)
-        met += 1
+    signal_chip(barrier, facing)
+
+    @pl.when(my_half == 0)
+    def _():
+        signal_rest(barrier)
+
     window_copy.start()
     table_copy.start()
 
@@ -170,11 +188,11 @@
             device_id_type=MESH,
         )
 
-    def place(hop):
-        return hop // 2 * 2 + lax.rem(hop + low, 2)
+    def place(hop, turn=0):
+        return lax.rem(hop // 2 + turn, 2) * 2 + lax.rem(hop + low, 2)
 
     def send_far(hop, g):
-        q = far_first + place(hop)
+        q = far_first + place(hop, chip * (1 - my_half) if g == 0 else 0)
         pack(q, g)
         row_copy(g, q, False).start()
         row_copy(g, q, True).start()
@@ -194,20 +212,32 @@
                 stage.at[g, q, mine], recv.at[g, side, ma], recv_sem.at[g, side, ma]
             ).start()
 
-    def each_hop(step):
+    def each_hop(step, first=0, end=half_ma):
         def body_of(hop, c):
             step(hop)
             return c
 
-        lax.fori_loop(0, half_ma, body_of, 0)
+        lax.fori_loop(first, end, body_of, 0)
+
+    pl.semaphore_wait(barrier, 4 + 6 * my_half)
+
+    @pl.when(my_half == 1)
+    def _():
+        signal_rest(late_sem)
+        signal(here_sem, lat, far)
 
     assign_copy.wait()
     rows_copy.wait()
-    pl.semaphore_wait(barrier, met)
-    pl.semaphore_signal(here_sem, inc=1, device_id=(lat, far), device_id_type=MESH)
-    each_hop(lambda hop: send_far(hop, 0))
+    each_hop(lambda hop: send_far(hop, 0), 0, half_ma // 2)
+
+    @pl.when(my_half == 0)
+    def _():
+        pl.semaphore_wait(late_sem, 6)
+        signal(here_sem, lat, far)
+
     pl.semaphore_wait(here_sem, 1)
     each_hop(lambda hop: send_near(hop, 0))
+    each_hop(lambda hop: send_far(hop, 0), half_ma // 2)
     each_hop(lambda hop: send_near(hop, 1))
     each_hop(lambda hop: send_far(hop, 1))
     window_copy.wait()
@@ -254,22 +284,25 @@
             device_id_type=MESH,
         )
 
-    def own_copy(c, e):
-        return pltpu.make_async_copy(
-            part.at[c, lat, e], out_ref.at[0, c, e], own_sem.at[c, e]
-        )
+    def own_copy(k):
+        return pltpu.make_async_copy(part.at[last, lat, k], out_ref.at[0, k], own_sem.at[k])
 
     def beside_copy(c, e):
-        return remote(c, e, 0, part.at[c, beside, e], out_ref.at[1, c, e], beside)
+        target = out_ref.at[1, e] if c == last else landed.at[0, c, e]
+        return remote(c, e, 0, part.at[c, beside, e], target, beside)
 
     def across_copy(c, e):
         source = part.at[c, across, e]
         if c == last:
-            return remote(c, e, 1, source, out_ref.at[3, c, e], across)
+            return remote(c, e, 1, source, out_ref.at[3, e], across)
         return remote(c, e, 1, source, relay.at[c, e], beside)
 
     def partner_copy(c, e):
-        return remote(c, e, 2, part.at[c, partner, e], out_ref.at[2, c, e], partner)
+        target = out_ref.at[2, e] if c == last else landed.at[1, c, e]
+        return remote(c, e, 2, part.at[c, partner, e], target, partner)
+
+    def sum_copy(c):
+        return pltpu.make_async_copy(total.at[c], sums_ref.at[c], sum_sem.at[c])
 
     def arrive(g, m):
         for ns in range(2):
@@ -296,10 +329,10 @@
                 across_copy(c, k).start()
             elif d is beside:
                 beside_copy(c, k).start()
-            elif d is lat:
-                own_copy(c, k).start()
+            elif c == last and d is partner:
+                partner_copy(c, k).start()
             elif c == last:
-                partner_copy(c, k).start()
+                own_copy(k).start()
 
     def multiply(c):
         g, j = chunks[c]
@@ -318,27 +351,24 @@
 
     even_lane = lax.broadcasted_iota(jnp.int32, (1, half_f), 1) < half_f // 2
 
-    def multiply_last():
+    def multiply_last(k):
         g = chunks[last][0]
-        for k in range(2):
-            core = lax.rem(low + k, 2)
-            members = [far_first + 2 * n + core for n in range(half_ma // 2)]
-            for m in members:
-                arrive(g, m)
-            north, south = (
-                jnp.concatenate([recv[g, ns, m] for m in members], axis=0).astype(F32)
-                for ns in range(2)
-            )
-            source = jnp.concatenate(
-                [source_of(g, e, north, south) for e in range(2)], axis=0
-            )
-            send_parts(
-                last,
-                k,
-                lambda d, source=source: jnp.where(
-                    even_lane, product(g, 0, d, source), product(g, 1, d, source)
-                ),
-            )
+        chips = half_ma // 2
+        first = far_first + chips * (1 - my_half if k == 0 else my_half)
+        for m in range(chips):
+            arrive(g, first + m)
+        north, south = (
+            recv[g, ns, pl.ds(first, chips)].reshape(half_f // 2, rows).astype(F32)
+            for ns in range(2)
+        )
+        source = jnp.concatenate([source_of(g, e, north, south) for e in range(2)], axis=0)
+        send_parts(
+            last,
+            k,
+            lambda d: jnp.where(
+                even_lane, product(g, 0, d, source), product(g, 1, d, source)
+            ),
+        )
 
     def pass_on(c):
         for e in range(2):
@@ -347,20 +377,32 @@
             part[c, partner, e] = total.astype(BF16)
             partner_copy(c, e).start()
 
-    multiply(0)
-    multiply(1)
-    pass_on(0)
-    pass_on(1)
-    multiply(2)
-    pass_on(2)
-    multiply_last()
-
-    for c in range(last + 1):
+    def finish(c):
         for e in range(2):
             beside_copy(c, e).wait_recv()
-            if c == last:
-                across_copy(c, e).wait_recv()
             partner_copy(c, e).wait_recv()
+            total[c, e] = (
+                part[c, lat, e].astype(F32)
+                + landed[0, c, e].astype(F32)
+                + landed[1, c, e].astype(F32)
+            )
+        sum_copy(c).start()
+
+    multiply(0)
+    multiply(2)
+    pass_on(0)
+    multiply(1)
+    pass_on(2)
+    multiply_last(0)
+    finish(0)
+    pass_on(1)
+    finish(2)
+    multiply_last(1)
+    finish(1)
+    for k in range(2):
+        beside_copy(last, k).wait_recv()
+        across_copy(last, k).wait_recv()
+        partner_copy(last, k).wait_recv()
 
     for g in range(groups_here):
 
@@ -379,56 +421,48 @@
             beside_copy(c, e).wait_send()
             across_copy(c, e).wait_send()
             partner_copy(c, e).wait_send()
-            own_copy(c, e).wait()
-
-
-def sum_kernel(ma_n, parts_ref, out_hbm, held, total, in_sem, out_sem):
-    chunk_count = held.shape[1]
-    groups_here = chunk_count // 2
-    half_f = held.shape[4]
+    for c in range(last):
+        sum_copy(c).wait()
+    for k in range(2):
+        own_copy(k).wait()
+
+
+def sum_kernel(ma_n, sums_ref, parts_ref, out_hbm, held, total, in_sem, out_sem):
+    last = sums_ref.shape[0]
+    groups_here = (last + 1) // 2
+    half_f = held.shape[3]
     my_half = lax.axis_index("ma") // (ma_n // 2)
-
-    def fetch(c):
-        terms = 4 if c == chunk_count - 1 else 3
-        return pltpu.make_async_copy(
-            parts_ref.at[pl.ds(0, terms), c], held.at[pl.ds(0, terms), c], in_sem.at[c]
-        )
 
     def store(c):
         at = pl.multiple_of(lax.rem(my_half + c // groups_here, 2) * half_f, 128)
         return pltpu.make_async_copy(
-            total.at[c],
+            total if c == last else sums_ref.at[c],
             out_hbm.at[c % groups_here, :, :, pl.ds(at, half_f)],
             out_sem.at[c],
         )
 
-    for c in range(chunk_count):
-        fetch(c).start()
-    for c in range(chunk_count):
-        fetch(c).wait()
-        value = held[0, c].astype(F32)
-        for k in range(1, 4 if c == chunk_count - 1 else 3):
-            value = value + held[k, c].astype(F32)
-        if c < chunk_count - 1:
-            total[c] = value
-        else:
-            swap = lax.rem(lax.axis_index("ma"), 2) == 1
-            lower = jnp.where(swap, value[1], value[0])
-            upper = jnp.where(swap, value[0], value[1])
-            width = half_f // 4
-            for e in range(2):
-                at = 2 * e * width
-                total[c, e] = jnp.concatenate(
-                    [
-                        lower[:, at : at + width],
-                        upper[:, at : at + width],
-                        lower[:, at + width : at + 2 * width],
-                        upper[:, at + width : at + 2 * width],
-                    ],
-                    axis=1,
-                )
+    fetch = pltpu.make_async_copy(parts_ref, held, in_sem)
+    fetch.start()
+    for c in range(last):
         store(c).start()
-    for c in range(chunk_count):
+    fetch.wait()
+    first, second = (
+        held[0, k].astype(F32)
+        + held[1, k].astype(F32)
+        + held[2, k].astype(F32)
+        + held[3, k].astype(F32)
+        for k in range(2)
+    )
+    lower = jnp.where(my_half == 0, second, first)
+    upper = jnp.where(my_half == 0, first, second)
+    width = half_f // 2
+    for e in range(2):
+        at = e * width
+        total[e] = jnp.concatenate(
+            [lower[:, at : at + width], upper[:, at : at + width]], axis=1
+        )
+    store(last).start()
+    for c in range(last + 1):
         store(c).wait()
 
 
@@ -443,11 +477,14 @@
     hbm = pl.BlockSpec(memory_space=pltpu.HBM)
     anywhere = pl.BlockSpec(memory_space=pl.ANY)
     dma = pltpu.SemaphoreType.DMA
-    parts = pl.pallas_call(
+    sums, parts = pl.pallas_call(
         functools.partial(fused_kernel, lat_n, ma_n),
-        out_shape=jax.ShapeDtypeStruct((4, chunks, 2, block, half_f), BF16),
+        out_shape=(
+            jax.ShapeDtypeStruct((chunks - 1, 2, block, half_f), F32),
+            jax.ShapeDtypeStruct((4, 2, block, half_f), BF16),
+        ),
         in_specs=[hbm, hbm, hbm, hbm],
-        out_specs=anywhere,
+        out_specs=(anywhere, anywhere),
         scratch_shapes=[
             pltpu.SMEM(assign.shape, jnp.int32),
             pltpu.SMEM(window.shape, jnp.int32),
@@ -458,12 +495,16 @@
             pltpu.VMEM((groups_here, 2, kcols, rows), BF16),
             pltpu.VMEM((chunks, lat_n, 2, block, half_f), BF16),
             pltpu.VMEM((chunks - 1, 2, block, half_f), BF16),
+            pltpu.VMEM((2, chunks - 1, 2, block, half_f), BF16),
+            pltpu.VMEM((chunks - 1, 2, block, half_f), F32),
             dma((groups_here, ma_n, 2)),
             dma((groups_here, 2, ma_n)),
             dma((chunks, 2, 3)),
             dma((chunks, 2, 3)),
-            dma((chunks, 2)),
+            dma((2,)),
+            dma((chunks - 1,)),
             dma((4,)),
+            pltpu.SemaphoreType.REGULAR,
             pltpu.SemaphoreType.REGULAR,
         ],
         compiler_params=pltpu.CompilerParams(
@@ -478,19 +519,19 @@
     return pl.pallas_call(
         functools.partial(sum_kernel, ma_n),
         out_shape=jax.ShapeDtypeStruct((groups_here, 2, block, fields), F32),
-        in_specs=[anywhere],
+        in_specs=[anywhere, anywhere],
         out_specs=hbm,
         scratch_shapes=[
             pltpu.VMEM(parts.shape, BF16),
-            pltpu.VMEM((chunks, 2, block, half_f), F32),
-            dma((chunks,)),
+            pltpu.VMEM((2, block, half_f), F32),
+            dma,
             dma((chunks,)),
         ],
         compiler_params=pltpu.CompilerParams(vmem_limit_bytes=16 * 2**20),
         cost_estimate=pl.CostEstimate(
             flops=parts.size, bytes_accessed=4 * parts.size, transcendentals=0
         ),
-    )(parts)
+    )(sums, parts)
 
 
 def fits_kernel(mesh, fourier, legendre):

time: 40.9 us -> 39.9 us (0.976)
  Pallas kernels: 40.7 us -> 39.5 us
    pallas_call x1, Pallas kernels: 39.3 us -> 38.5 us  [fused_on_device(): pl.pallas_call(functools.partial(fused_kernel, lat_n, ma_n), out_shape=(j...]
    pallas_call x1, Pallas kernels: 1.42 us -> 0.99 us  [fused_on_device(): pl.pallas_call(functools.partial(sum_kernel, ma_n), out_shape=jax.ShapeDt...]
where the time goes in v3:
time: 39.9 us; the launch traced here: 39.5 us
  Pallas kernels  39.5 us (99%)
    pallas_call x1, Pallas kernels, fused_on_device(): pl.pallas_call(functools.partial(fused_kernel, lat_n, ma_n), out_shape=(j...  38.5 us
    pallas_call x1, Pallas kernels, fused_on_device(): pl.pallas_call(functools.partial(sum_kernel, ma_n), out_shape=jax.ShapeDt...  0.99 us

profile of v3, /device:TPU:25, one launch (start us, length us, event | category | flops | bytes accessed | tf_op | source)
XLA Modules:
  0.0 39.5 jit_solution(14242922109408039123)
XLA Ops:
  0.0 38.5 %shard_map.46 = (f32[3,2,160,128]{3,2,1,0:T(8,128)S(1)}, bf16[4,2,160,128]{3,2,1,0:T(8,128)(2,1)S(1)}) custom-call(s32[16]{0:T(128)} %assign_hbm.1, s32[16]{0:T(128)} %window_hbm.1, bf16[16,2,32,640]{3,2,1,0:T(8,128)(2,1)} %four_hbm.1, bf16[2,320,2,640]{3,2,1,0:T(2,128)(2,1)} %leg_hbm.1), custom_call_target="tpu_custom_call" | custom-call | flops 1677721600 | bytes 2949120 | tf_op jit(solution)/shard_map/pallas_call | solution.py:480
  38.5 1.0 %shard_map.47 = f32[2,2,160,256]{3,2,1,0:T(8,128)} custom-call(f32[3,2,160,128]{3,2,1,0:T(8,128)S(1)} %get-tuple-element.7.sums_ref, bf16[4,2,160,128]{3,2,1,0:T(8,128)(2,1)S(1)} %get-tuple-element.8.parts_ref), custom_call_target="tpu_custom_call" | custom-call | flops 163840 | bytes 655360 | tf_op jit(solution)/shard_map/pallas_call | solution.py:519

commit v4 on v3

--- a/solution.py
+++ b/solution.py
@@ -135,14 +135,14 @@
     assign_copy.start()
     rows_copy.start()
 
-    far = lax.rem(ma + half_ma, ma_n)
     far_first = (1 - my_half) * half_ma
     near_first = my_half * half_ma
     low = lax.rem(ma, 2)
 
     chip = lax.rem(ma // 2, 2)
-    facing = far_first + 2 * chip
-    other = far_first + 2 * (1 - chip)
+    facing = far_first + 2 * (1 - chip)
+    other = far_first + 2 * chip
+    far = facing + low
 
     def signal(semaphore, there, q):
         pl.semaphore_signal(semaphore, inc=1, device_id=(there, q), device_id_type=MESH)
@@ -192,7 +192,7 @@
         return lax.rem(hop // 2 + turn, 2) * 2 + lax.rem(hop + low, 2)
 
     def send_far(hop, g):
-        q = far_first + place(hop, chip * (1 - my_half) if g == 0 else 0)
+        q = far_first + place(hop, (1 - chip) * (1 - my_half) if g == 0 else 0)
         pack(q, g)
         row_copy(g, q, False).start()
         row_copy(g, q, True).start()
@@ -399,11 +399,6 @@
     finish(2)
     multiply_last(1)
     finish(1)
-    for k in range(2):
-        beside_copy(last, k).wait_recv()
-        across_copy(last, k).wait_recv()
-        partner_copy(last, k).wait_recv()
-
     for g in range(groups_here):
 
         def sent(q, c, g=g):
@@ -416,18 +411,20 @@
             return c
 
         lax.fori_loop(0, ma_n, sent, 0)
-    for c in range(last + 1):
+    for c in range(last):
         for e in range(2):
             beside_copy(c, e).wait_send()
             across_copy(c, e).wait_send()
             partner_copy(c, e).wait_send()
-    for c in range(last):
         sum_copy(c).wait()
     for k in range(2):
         own_copy(k).wait()
-
-
-def sum_kernel(ma_n, sums_ref, parts_ref, out_hbm, held, total, in_sem, out_sem):
+        beside_copy(last, k).wait()
+        across_copy(last, k).wait()
+        partner_copy(last, k).wait()
+
+
+def sum_kernel(ma_n, sums_ref, held, out_hbm, total, out_sem):
     last = sums_ref.shape[0]
     groups_here = (last + 1) // 2
     half_f = held.shape[3]
@@ -441,11 +438,8 @@
             out_sem.at[c],
         )
 
-    fetch = pltpu.make_async_copy(parts_ref, held, in_sem)
-    fetch.start()
     for c in range(last):
         store(c).start()
-    fetch.wait()
     first, second = (
         held[0, k].astype(F32)
         + held[1, k].astype(F32)
@@ -519,12 +513,10 @@
     return pl.pallas_call(
         functools.partial(sum_kernel, ma_n),
         out_shape=jax.ShapeDtypeStruct((groups_here, 2, block, fields), F32),
-        in_specs=[anywhere, anywhere],
+        in_specs=[anywhere, pl.BlockSpec(memory_space=pltpu.VMEM)],
         out_specs=hbm,
         scratch_shapes=[
-            pltpu.VMEM(parts.shape, BF16),
             pltpu.VMEM((2, block, half_f), F32),
-            dma,
             dma((chunks,)),
         ],
         compiler_params=pltpu.CompilerParams(vmem_limit_bytes=16 * 2**20),

time: 39.9 us -> 39.1 us (0.980); the launches traced: 39.5 us -> 38.3 us
  Pallas kernels: 39.5 us -> 38.3 us
    pallas_call x1, Pallas kernels: 38.5 us -> 37.4 us  [fused_on_device(): pl.pallas_call(functools.partial(fused_kernel, lat_n, ma_n), out_shape=(j...]
where the time goes in v4:
time: 39.1 us; the launch traced here: 38.3 us
  Pallas kernels  38.3 us (98%)
    pallas_call x1, Pallas kernels, fused_on_device(): pl.pallas_call(functools.partial(fused_kernel, lat_n, ma_n), out_shape=(j...  37.4 us
    pallas_call x1, Pallas kernels, fused_on_device(): pl.pallas_call(functools.partial(sum_kernel, ma_n), out_shape=jax.ShapeDt...  0.9 us

profile of v4, /device:TPU:25, one launch (start us, length us, event | category | flops | bytes accessed | tf_op | source)
XLA Modules:
  0.0 38.3 jit_solution(3159235460079583999)
XLA Ops:
  0.0 37.4 %shard_map.46 = (f32[3,2,160,128]{3,2,1,0:T(8,128)S(1)}, bf16[4,2,160,128]{3,2,1,0:T(8,128)(2,1)S(1)}) custom-call(s32[16]{0:T(128)} %assign_hbm.1, s32[16]{0:T(128)} %window_hbm.1, bf16[16,2,32,640]{3,2,1,0:T(8,128)(2,1)} %four_hbm.1, bf16[2,320,2,640]{3,2,1,0:T(2,128)(2,1)} %leg_hbm.1), custom_call_target="tpu_custom_call" | custom-call | flops 1677721600 | bytes 2949120 | tf_op jit(solution)/shard_map/pallas_call | solution.py:474
  37.4 0.9 %shard_map.47 = f32[2,2,160,256]{3,2,1,0:T(8,128)} custom-call(f32[3,2,160,128]{3,2,1,0:T(8,128)S(1)} %get-tuple-element.7.sums_ref, bf16[4,2,160,128]{3,2,1,0:T(8,128)(2,1)S(1)} %get-tuple-element.8.held), custom_call_target="tpu_custom_call" | custom-call | flops 163840 | bytes 655360 | tf_op jit(solution)/shard_map/pallas_call | solution.py:513

commit v5 on v4

--- a/solution.py
+++ b/solution.py
@@ -188,11 +188,14 @@
             device_id_type=MESH,
         )
 
-    def place(hop, turn=0):
-        return lax.rem(hop // 2 + turn, 2) * 2 + lax.rem(hop + low, 2)
+    def place(hop, turn=0, core=low):
+        return lax.rem(hop // 2 + turn, 2) * 2 + lax.rem(hop + core, 2)
 
     def send_far(hop, g):
-        q = far_first + place(hop, (1 - chip) * (1 - my_half) if g == 0 else 0)
+        if g == 0:
+            q = far_first + place(hop, (1 - chip) * (1 - my_half))
+        else:
+            q = far_first + place(hop, 0, 0)
         pack(q, g)
         row_copy(g, q, False).start()
         row_copy(g, q, True).start()
@@ -284,22 +287,35 @@
             device_id_type=MESH,
         )
 
+    half_block = block // 2
+
+    def piece_of(ref, c, k):
+        if c < last or k == 0:
+            return ref.at[k]
+        return ref.at[1, pl.ds((k - 1) * half_block, half_block)]
+
     def own_copy(k):
-        return pltpu.make_async_copy(part.at[last, lat, k], out_ref.at[0, k], own_sem.at[k])
-
-    def beside_copy(c, e):
-        target = out_ref.at[1, e] if c == last else landed.at[0, c, e]
-        return remote(c, e, 0, part.at[c, beside, e], target, beside)
-
-    def across_copy(c, e):
-        source = part.at[c, across, e]
+        return pltpu.make_async_copy(
+            piece_of(part.at[last, lat], last, k),
+            piece_of(out_ref.at[0], last, k),
+            own_sem.at[k],
+        )
+
+    def beside_copy(c, k):
+        target = out_ref.at[1] if c == last else landed.at[0, c]
+        source = piece_of(part.at[c, beside], c, k)
+        return remote(c, k, 0, source, piece_of(target, c, k), beside)
+
+    def across_copy(c, k):
+        source = piece_of(part.at[c, across], c, k)
         if c == last:
-            return remote(c, e, 1, source, out_ref.at[3, e], across)
-        return remote(c, e, 1, source, relay.at[c, e], beside)
-
-    def partner_copy(c, e):
-        target = out_ref.at[2, e] if c == last else landed.at[1, c, e]
-        return remote(c, e, 2, part.at[c, partner, e], target, partner)
+            return remote(c, k, 1, source, piece_of(out_ref.at[3], c, k), across)
+        return remote(c, k, 1, source, relay.at[c, k], beside)
+
+    def partner_copy(c, k):
+        target = out_ref.at[2] if c == last else landed.at[1, c]
+        source = piece_of(part.at[c, partner], c, k)
+        return remote(c, k, 2, source, piece_of(target, c, k), partner)
 
     def sum_copy(c):
         return pltpu.make_async_copy(total.at[c], sums_ref.at[c], sum_sem.at[c])
@@ -324,7 +340,10 @@
 
     def send_parts(c, k, value):
         for d in (across, beside, partner, lat):
-            part[c, d, k] = value(d).astype(BF16)
+            if c < last or k == 0:
+                part[c, d, k] = value(d).astype(BF16)
+            else:
+                part[c, d, 1, pl.ds((k - 1) * half_block, half_block)] = value(d).astype(BF16)
             if d is across:
                 across_copy(c, k).start()
             elif d is beside:
@@ -349,12 +368,14 @@
             source = source_of(g, e, north, south)
             send_parts(c, e, lambda d, e=e, source=source: product(g, e, d, source))
 
-    even_lane = lax.broadcasted_iota(jnp.int32, (1, half_f), 1) < half_f // 2
-
-    def multiply_last(k):
+    lanes = lax.broadcasted_iota(jnp.int32, (1, half_f), 1)
+    left = lanes < half_f // 2
+    even_lane = lax.rem(lanes, half_f // 2) < half_f // 4
+
+    def multiply_outer():
         g = chunks[last][0]
         chips = half_ma // 2
-        first = far_first + chips * (1 - my_half if k == 0 else my_half)
+        first = far_first + chips * (1 - my_half)
         for m in range(chips):
             arrive(g, first + m)
         north, south = (
@@ -364,11 +385,22 @@
         source = jnp.concatenate([source_of(g, e, north, south) for e in range(2)], axis=0)
         send_parts(
             last,
-            k,
-            lambda d: jnp.where(
-                even_lane, product(g, 0, d, source), product(g, 1, d, source)
-            ),
-        )
+            0,
+            lambda d: jnp.where(left, product(g, 0, d, source), product(g, 1, d, source)),
+        )
+
+    def multiply_inner(k):
+        g = chunks[last][0]
+        m = far_first + half_ma // 2 * my_half + 2 - k
+        arrive(g, m)
+        north, south = (recv[g, ns, m].astype(F32) for ns in range(2))
+        source = jnp.concatenate([source_of(g, e, north, south) for e in range(2)] * 2, axis=0)
+
+        def value(d):
+            both = jnp.where(even_lane, product(g, 0, d, source), product(g, 1, d, source))
+            return jnp.where(left, both[:half_block], both[half_block:])
+
+        send_parts(last, k, value)
 
     def pass_on(c):
         for e in range(2):
@@ -393,11 +425,12 @@
     pass_on(0)
     multiply(1)
     pass_on(2)
-    multiply_last(0)
+    multiply_outer()
     finish(0)
     pass_on(1)
     finish(2)
-    multiply_last(1)
+    multiply_inner(1)
+    multiply_inner(2)
     finish(1)
     for g in range(groups_here):
 
@@ -417,7 +450,7 @@
             across_copy(c, e).wait_send()
             partner_copy(c, e).wait_send()
         sum_copy(c).wait()
-    for k in range(2):
+    for k in range(3):
         own_copy(k).wait()
         beside_copy(last, k).wait()
         across_copy(last, k).wait()
@@ -447,13 +480,21 @@
         + held[3, k].astype(F32)
         for k in range(2)
     )
-    lower = jnp.where(my_half == 0, second, first)
-    upper = jnp.where(my_half == 0, first, second)
-    width = half_f // 2
+    rows = second.shape[0] // 2
+    core1, core0 = second[:rows], second[rows:]
+    width = half_f // 4
     for e in range(2):
-        at = e * width
+        inner = jnp.concatenate(
+            [
+                jnp.concatenate([core0[:, at : at + width], core1[:, at : at + width]], axis=1)
+                for at in (e * width, (2 + e) * width)
+            ],
+            axis=0,
+        )
+        outer = first[:, 2 * e * width : 2 * (e + 1) * width]
         total[e] = jnp.concatenate(
-            [lower[:, at : at + width], upper[:, at : at + width]], axis=1
+            [jnp.where(my_half == 0, inner, outer), jnp.where(my_half == 0, outer, inner)],
+            axis=1,
         )
     store(last).start()
     for c in range(last + 1):
@@ -493,9 +534,9 @@
             pltpu.VMEM((chunks - 1, 2, block, half_f), F32),
             dma((groups_here, ma_n, 2)),
             dma((groups_here, 2, ma_n)),
-            dma((chunks, 2, 3)),
-            dma((chunks, 2, 3)),
-            dma((2,)),
+            dma((chunks, 3, 3)),
+            dma((chunks, 3, 3)),
+            dma((3,)),
             dma((chunks - 1,)),
             dma((4,)),
             pltpu.SemaphoreType.REGULAR,
@@ -539,7 +580,7 @@
         and fields_here % 16 == 0
         and (fields_here * ma_n) % 256 == 0
         and (2 * pair) % 128 == 0
-        and block % 16 == 0
+        and block % 32 == 0
         and legendre.shape[3] % 128 == 0
     )
 

time: 39.1 us -> 38.4 us (0.982)
  Pallas kernels: 38.3 us -> 37.9 us
    pallas_call x1, Pallas kernels: 37.4 us -> 36.9 us  [fused_on_device(): pl.pallas_call(functools.partial(fused_kernel, lat_n, ma_n), out_shape=(j...]
where the time goes in v5:
time: 38.4 us; the launch traced here: 37.9 us
  Pallas kernels  37.9 us (99%)
    pallas_call x1, Pallas kernels, fused_on_device(): pl.pallas_call(functools.partial(fused_kernel, lat_n, ma_n), out_shape=(j...  36.9 us
    pallas_call x1, Pallas kernels, fused_on_device(): pl.pallas_call(functools.partial(sum_kernel, ma_n), out_shape=jax.ShapeDt...  0.96 us

profile of v5, /device:TPU:25, one launch (start us, length us, event | category | flops | bytes accessed | tf_op | source)
XLA Modules:
  0.0 37.9 jit_solution(11621575971245382957)
XLA Ops:
  0.0 36.9 %shard_map.46 = (f32[3,2,160,128]{3,2,1,0:T(8,128)S(1)}, bf16[4,2,160,128]{3,2,1,0:T(8,128)(2,1)S(1)}) custom-call(s32[16]{0:T(128)} %assign_hbm.1, s32[16]{0:T(128)} %window_hbm.1, bf16[16,2,32,640]{3,2,1,0:T(8,128)(2,1)} %four_hbm.1, bf16[2,320,2,640]{3,2,1,0:T(2,128)(2,1)} %leg_hbm.1), custom_call_target="tpu_custom_call" | custom-call | flops 1677721600 | bytes 2949120 | tf_op jit(solution)/shard_map/pallas_call | solution.py:515
  36.9 1.0 %shard_map.47 = f32[2,2,160,256]{3,2,1,0:T(8,128)} custom-call(f32[3,2,160,128]{3,2,1,0:T(8,128)S(1)} %get-tuple-element.7.sums_ref, bf16[4,2,160,128]{3,2,1,0:T(8,128)(2,1)S(1)} %get-tuple-element.8.held), custom_call_target="tpu_custom_call" | custom-call | flops 163840 | bytes 655360 | tf_op jit(solution)/shard_map/pallas_call | solution.py:554

commit v6 on v5

--- a/solution.py
+++ b/solution.py
@@ -152,17 +152,14 @@
             for there in (lat, partner):
                 signal(semaphore, there, first + m)
 
-    def signal_rest(semaphore):
-        signal_chip(semaphore, other)
-        for there in (beside, across):
-            signal(semaphore, there, far)
-
     barrier = pltpu.get_barrier_semaphore()
     signal_chip(barrier, facing)
 
     @pl.when(my_half == 0)
     def _():
-        signal_rest(barrier)
+        signal_chip(barrier, other)
+        for there in (beside, across):
+            signal(barrier, there, ma)
 
     window_copy.start()
     table_copy.start()
@@ -222,12 +219,16 @@
 
         lax.fori_loop(first, end, body_of, 0)
 
-    pl.semaphore_wait(barrier, 4 + 6 * my_half)
+    pl.semaphore_wait(barrier, 6 + 2 * my_half)
 
     @pl.when(my_half == 1)
     def _():
-        signal_rest(late_sem)
+        signal_chip(late_sem, other)
         signal(here_sem, lat, far)
+
+    @pl.when(my_half == 0)
+    def _():
+        signal(late_sem, beside, ma)
 
     assign_copy.wait()
     rows_copy.wait()
@@ -235,7 +236,7 @@
 
     @pl.when(my_half == 0)
     def _():
-        pl.semaphore_wait(late_sem, 6)
+        pl.semaphore_wait(late_sem, 5)
         signal(here_sem, lat, far)
 
     pl.semaphore_wait(here_sem, 1)
@@ -425,9 +426,18 @@
     pass_on(0)
     multiply(1)
     pass_on(2)
+
+    @pl.when(chip == 1)
+    def _():
+        pass_on(1)
+
     multiply_outer()
     finish(0)
-    pass_on(1)
+
+    @pl.when(chip == 0)
+    def _():
+        pass_on(1)
+
     finish(2)
     multiply_inner(1)
     multiply_inner(2)

time: 38.4 us -> 38.3 us (level)
  no operation moved by 1% of the time
where the time goes in v6:
time: 38.3 us; the launch traced here: 37.9 us
  Pallas kernels  37.9 us (99%)
    pallas_call x1, Pallas kernels, fused_on_device(): pl.pallas_call(functools.partial(fused_kernel, lat_n, ma_n), out_shape=(j...  36.9 us
    pallas_call x1, Pallas kernels, fused_on_device(): pl.pallas_call(functools.partial(sum_kernel, ma_n), out_shape=jax.ShapeDt...  0.96 us

profile of v6, /device:TPU:25, one launch (start us, length us, event | category | flops | bytes accessed | tf_op | source)
XLA Modules:
  0.0 37.9 jit_solution(9423797975633347140)
XLA Ops:
  0.0 36.9 %shard_map.46 = (f32[3,2,160,128]{3,2,1,0:T(8,128)S(1)}, bf16[4,2,160,128]{3,2,1,0:T(8,128)(2,1)S(1)}) custom-call(s32[16]{0:T(128)} %assign_hbm.1, s32[16]{0:T(128)} %window_hbm.1, bf16[16,2,32,640]{3,2,1,0:T(8,128)(2,1)} %four_hbm.1, bf16[2,320,2,640]{3,2,1,0:T(2,128)(2,1)} %leg_hbm.1), custom_call_target="tpu_custom_call" | custom-call | flops 1677721600 | bytes 2949120 | tf_op jit(solution)/shard_map/pallas_call | solution.py:525
  36.9 1.0 %shard_map.47 = f32[2,2,160,256]{3,2,1,0:T(8,128)} custom-call(f32[3,2,160,128]{3,2,1,0:T(8,128)S(1)} %get-tuple-element.7.sums_ref, bf16[4,2,160,128]{3,2,1,0:T(8,128)(2,1)S(1)} %get-tuple-element.8.held), custom_call_target="tpu_custom_call" | custom-call | flops 163840 | bytes 655360 | tf_op jit(solution)/shard_map/pallas_call | solution.py:564
